TPU v7x, 32 devices: a whole 2x2x4 slice. The times are simulated.
32 devices in a mesh: seq: 8 (over z, x), grp: 4 (over y, core).
Axes of the slice: x: 2, y: 2, z: 4, core: 2. Of those that a mesh axis runs over, the one named last changes fastest.
Arguments:
- linear_query: bfloat16 [4096, 256], P(('grp', 'seq')), parts along dimension 0, may hold values from -6 to 6
- linear_key: bfloat16 [4096, 256], P(('grp', 'seq')), parts along dimension 0, may hold values from -16 to 16
- values: bfloat16 [4096, 2048], P(('grp', 'seq')), parts along dimension 0, may hold values from -6 to 6
- window_query: bfloat16 [4096, 2048], P(('grp', 'seq')), parts along dimension 0, may hold values from -5 to 5
- window_key: bfloat16 [4096, 2048], P(('grp', 'seq')), parts along dimension 0, may hold values from -5 to 5
Outputs:
- linear_out: float32 [4096, 2048], P(('grp', 'seq')), parts along dimension 0
- window_out: bfloat16 [4096, 2048], P(('grp', 'seq')), parts along dimension 0
There are 4 independent parts, one for each index of `grp`. A program takes and returns all parts, laid end to end along the dimension named above; each array names one. Nothing has to cross between parts.
All inputs are finite; a program needn't handle non-finite values.
Results may differ from a plain program's by a relative error of at most 0.0085.
Values may be sent and summed in bfloat16 or wider, within the bound.
A program may use at most 64 MiB of HBM per device.

v0:
```python
import jax
import jax.numpy as jnp
import numpy as np
from jax import lax
from jax.sharding import PartitionSpec as P

FEAT = 16
WINDOW = 256


PRECISE = lax.Precision.HIGHEST
HALF_ROOT = 0.7071067811865476


def passed_along(block, axis, distance):
    devices = range(lax.axis_size(axis))
    route = [(i - distance, i) for i in devices if i - distance in devices]
    return lax.ppermute(block, axis, route)


def pair_features(scaled):
    row_count, head_count, feat_count = scaled.shape
    columns = jnp.transpose(scaled, (1, 2, 0))
    lower_index, upper_index = np.triu_indices(feat_count)
    identity = np.eye(feat_count, dtype=np.float32)
    pick_lower = jnp.asarray(identity[:, lower_index])
    pick_upper = jnp.asarray(identity[:, upper_index])
    pair_weight = jnp.asarray(
        np.where(lower_index == upper_index, HALF_ROOT, 1.0).astype(np.float32)
    )
    left_side = jnp.einsum("hfr,fp->hpr", columns, pick_lower, precision=PRECISE)
    right_side = jnp.einsum("hfr,fp->hpr", columns, pick_upper, precision=PRECISE)
    paired = left_side * right_side * pair_weight[None, :, None]
    return jnp.concatenate(
        [jnp.ones((head_count, 1, row_count), jnp.float32), columns, paired], axis=1
    )


def on_device(linear_query, linear_key, values, window_query, window_key):
    row_count = values.shape[0]
    head_count = linear_query.shape[1] // FEAT
    value_width = values.shape[1] // head_count
    seq_count = lax.axis_size("seq")
    seq_index = lax.axis_index("seq")
    start_pos = seq_index * row_count
    query_scaled = (linear_query.astype(jnp.float32) * FEAT ** (-0.25)).reshape(
        row_count, head_count, FEAT
    )
    key_scaled = (linear_key.astype(jnp.float32) * FEAT ** (-0.25)).reshape(
        row_count, head_count, FEAT
    )
    value_heads = values.astype(jnp.float32).reshape(row_count, head_count, value_width)
    query_feats = pair_features(query_scaled)
    key_feats = pair_features(key_scaled)
    local_state = jnp.einsum("hpr,rhv->hpv", key_feats, value_heads, precision=PRECISE)
    local_norm = jnp.sum(key_feats, axis=2)
    running_state = local_state
    running_norm = local_norm
    distance = 1
    while distance < seq_count:
        arrived = passed_along((running_state, running_norm), "seq", distance)
        running_state = running_state + arrived[0]
        running_norm = running_norm + arrived[1]
        distance = distance * 2
    prior_state = running_state - local_state
    prior_norm = running_norm - local_norm
    causal = jnp.arange(row_count)[:, None] >= jnp.arange(row_count)[None, :]
    inner_prod = jnp.einsum("thf,jhf->htj", query_scaled, key_scaled, precision=PRECISE)
    kernel = jnp.where(causal[None], 1.0 + inner_prod + 0.5 * inner_prod * inner_prod, 0.0)
    numerator = jnp.einsum("htj,jhv->thv", kernel, value_heads, precision=PRECISE) + jnp.einsum(
        "hpt,hpv->thv", query_feats, prior_state, precision=PRECISE
    )
    denominator = jnp.sum(kernel, axis=2).T + jnp.einsum(
        "hpt,hp->th", query_feats, prior_norm, precision=PRECISE
    )
    linear_out = (numerator / denominator[:, :, None]).reshape(row_count, head_count * value_width)
    span_rows = min(row_count, WINDOW)
    reach_count = -(-WINDOW // row_count)
    moved_keys = []
    moved_values = []
    for distance in range(1, reach_count + 1):
        arrived = passed_along((window_key, values), "seq", distance)
        moved_keys.append(arrived[0])
        moved_values.append(arrived[1])
    all_keys = jnp.concatenate(moved_keys[::-1] + [window_key], axis=0)
    all_values = jnp.concatenate(moved_values[::-1] + [values], axis=0)
    key_count = all_keys.shape[0]
    query_pos = start_pos + jnp.arange(row_count, dtype=jnp.int32)
    key_pos = start_pos - reach_count * span_rows + jnp.arange(key_count, dtype=jnp.int32)
    allowed = (
        (key_pos[None, :] <= query_pos[:, None])
        & (key_pos[None, :] > query_pos[:, None] - WINDOW)
        & (key_pos[None, :] >= 0)
    )
    scores = jnp.einsum(
        "thd,jhd->htj",
        window_query.reshape(row_count, head_count, value_width),
        all_keys.reshape(key_count, head_count, value_width),
        preferred_element_type=jnp.float32,
    ) * value_width ** (-0.5)
    masked = jnp.where(allowed[None], scores, -jnp.inf)
    largest = jnp.max(masked, axis=2, keepdims=True)
    exponent = jnp.exp(masked - largest)
    weights = (exponent / jnp.sum(exponent, axis=2, keepdims=True)).astype(jnp.bfloat16)
    mixed = jnp.einsum(
        "htj,jhv->thv",
        weights,
        all_values.reshape(key_count, head_count, value_width),
        preferred_element_type=jnp.float32,
    )
    window_out = mixed.astype(jnp.bfloat16).reshape(row_count, head_count * value_width)
    return (linear_out, window_out)


def solution(mesh):
    return jax.shard_map(
        on_device,
        mesh=mesh,
        in_specs=(
            P(("grp", "seq"), None),
            P(("grp", "seq"), None),
            P(("grp", "seq"), None),
            P(("grp", "seq"), None),
            P(("grp", "seq"), None),
        ),
        out_specs=(P(("grp", "seq"), None), P(("grp", "seq"), None)),
        check_vma=False,
    )
```

profile of v0, /device:TPU:24, one launch (start us, length us, event | category | flops | bytes accessed | tf_op | source)
XLA Modules:
  0.0 185.7 jit_solution(6499836618811250640)
XLA Ops:
  0.7 2.1 %copy.67 = bf16[128,2048]{0,1:T(8,128)(2,1)} copy(bf16[128,2048]{1,0:T(8,128)(2,1)} %param.15) | data formatting | bytes 1048576 | tf_op args[4]
  4.1 3.4 %collective-permute-start.9 = (bf16[128,2048]{0,1:T(8,128)(2,1)}, bf16[128,2048]{0,1:T(8,128)(2,1)}, u32[]{:S(2)}, u32[]{:S(2)}) collective-permute-start(bf16[128,2048]{0,1:T(8,128)(2,1)} %copy.67), channel_id=1, source_target_pairs={{0,4},{4,8},{8,12},{12,16},{16,20},{20,24},{24,28},{1,5},{5,9},{9,... | collective-permute-start | bytes 1572872 | tf_op jit(solution)/shard_map/ppermute | solution.py:18
  11.5 1.9 %collective-permute-start.3 = (f32[16,153]{1,0:T(8,128)S(1)}, f32[16,153]{1,0:T(8,128)S(1)}, u32[]{:S(2)}, u32[]{:S(2)}) collective-permute-start(f32[16,153]{1,0:T(8,128)S(1)} %fusion.17), channel_id=1, source_target_pairs={{0,4},{4,8},{8,12},{12,16},{16,20},{20,24},{24,28},{1,5},{5,9},{9,... | collective-permute-start | bytes 29384 | tf_op jit(solution)/shard_map/ppermute | solution.py:18
  13.4 1.3 collective-permute-start.6
  15.6 1.8 copy.63
  17.4 1.9 %collective-permute-start = (f32[16,153,128]{2,0,1:T(8,128)}, f32[16,153,128]{2,0,1:T(8,128)}, u32[]{:S(2)}, u32[]{:S(2)}) collective-permute-start(f32[16,153,128]{2,0,1:T(8,128)} %copy.63), channel_id=1, source_target_pairs={{0,4},{4,8},{8,12},{12,16},{16,20},{20,24},{24,28},{1,5},{5,9},{9,... | collective-permute-start | bytes 3760136 | tf_op jit(solution)/shard_map/ppermute | solution.py:18
  20.6 1.8 fusion.35
  23.6 1.7 convolution_bitcast_fusion.1
  25.3 6.9 %collective-permute-done.3 = f32[16,153]{1,0:T(8,128)S(1)} collective-permute-done((f32[16,153]{1,0:T(8,128)S(1)}, f32[16,153]{1,0:T(8,128)S(1)}, u32[]{:S(2)}, u32[]{:S(2)}) %collective-permute-start.3) | collective-permute-done | bytes 9824 | tf_op jit(solution)/shard_map/ppermute | solution.py:18
  33.5 4.3 %collective-permute-done.4 = f32[16,153]{1,0:T(8,128)S(1)} collective-permute-done((f32[16,153]{1,0:T(8,128)S(1)}, f32[16,153]{1,0:T(8,128)S(1)}, u32[]{:S(2)}, u32[]{:S(2)}) %collective-permute-start.4) | collective-permute-done | bytes 9824 | tf_op jit(solution)/shard_map/ppermute | solution.py:18
  39.1 30.3 %collective-permute-done = f32[16,153,128]{2,0,1:T(8,128)} collective-permute-done((f32[16,153,128]{2,0,1:T(8,128)}, f32[16,153,128]{2,0,1:T(8,128)}, u32[]{:S(2)}, u32[]{:S(2)}) %collective-permute-start) | collective-permute-done | bytes 1253408 | tf_op jit(solution)/shard_map/ppermute | solution.py:18
  69.4 3.1 %copy_add_fusion = f32[16,153,128]{2,0,1:T(8,128)} fusion(f32[16,153,128]{2,0,1:T(8,128)} %collective-permute-done, f32[16,153,128]{2,1,0:T(8,128)S(1)} %fusion.18), kind=kLoop, calls=%fused_computation.62 | loop fusion | flops 313344 | bytes 3760128 | tf_op jit(solution)/shard_map/add | solution.py:62
  72.5 1.4 collective-permute-start.1
  74.7 4.0 %collective-permute-start.7 = (bf16[128,2048]{1,0:T(8,128)(2,1)S(1)}, bf16[128,2048]{1,0:T(8,128)(2,1)S(1)}, u32[]{:S(2)}, u32[]{:S(2)}) collective-permute-start(bf16[128,2048]{1,0:T(8,128)(2,1)S(1)} %copy-done.1), channel_id=1, source_target_pairs={{0,4},{4,8},{8,12},{12,16},{16,20},{20,24},{24,28},{1,5},{5,9},{9,... | collective-permute-start | bytes 1572872 | tf_op jit(solution)/shard_map/ppermute | solution.py:18
  80.0 35.4 %collective-permute-done.7 = bf16[128,2048]{1,0:T(8,128)(2,1)S(1)} collective-permute-done((bf16[128,2048]{1,0:T(8,128)(2,1)S(1)}, bf16[128,2048]{1,0:T(8,128)(2,1)S(1)}, u32[]{:S(2)}, u32[]{:S(2)}) %collective-permute-start.7) | collective-permute-done | bytes 524320 | tf_op jit(solution)/shard_map/ppermute | solution.py:18
  116.6 1.6 copy.66
  118.2 1.6 pad_maximum_fusion.1
  119.8 1.8 add.73
  125.2 1.4 fusion.13
  126.6 2.0 %copy.74 = bf16[128,2048]{1,0:T(8,128)(2,1)} copy(bf16[128,2048]{0,1:T(8,128)(2,1)} %bitcast.89) | data formatting | bytes 1048576
  128.6 50.0 %collective-permute-done.2 = f32[16,153,128]{2,0,1:T(8,128)} collective-permute-done((f32[16,153,128]{2,0,1:T(8,128)S(1)}, f32[16,153,128]{2,0,1:T(8,128)}, u32[]{:S(2)}, u32[]{:S(2)}) %collective-permute-start.2) | collective-permute-done | bytes 1253408 | tf_op jit(solution)/shard_map/ppermute | solution.py:18
  178.6 2.1 %add_subtract_fusion = f32[16,153,128]{2,0,1:T(8,128)S(1)} fusion(f32[16,153,128]{2,0,1:T(8,128)S(1)} %add.73, f32[16,153,128]{2,0,1:T(8,128)} %collective-permute-done.2, f32[16,153,128]{2,1,0:T(8,128)S(1)} %fusion.18), kind=kLoop, calls=%fused_computation.26 | loop fusion | flops 626688 | bytes 5013504 | tf_op jit(solution)/shard_map/sub | solution.py:65
  180.7 3.7 %fusion.11 = f32[128,16,128]{0,2,1:T(8,128)S(1)} fusion(f32[128,16,128]{0,2,1:T(8,128)S(1)} %copy-done.6, f32[16,153,128]{2,0,1:T(8,128)S(1)} %add_subtract_fusion, f32[16,136,128]{2,1,0:T(8,128)S(1)} %copy-done.5, f32[16,16,128]{2,1,0:T(8,128)S(1)} %bitcast.87, f32[153]{0:T(256)S(1)} %pad.9.clone, f32[128,16]{0,1:T(8,128)S(1)} %add_bitcast_fusion), kind=kOutput, calls=%fused_computation.21 | convolution fusion | flops 482447360 | bytes 4604516 | tf_op jit(solution)/shard_map/hpt,hpv->thv/dot_general | solution.py:70
  184.4 1.3 copy.73
  (57 shorter events, 17.8 us)
Async XLA Ops:
  0.6 122.3 %copy-start = (bf16[128,2048]{1,0:T(8,128)(2,1)S(1)}, bf16[128,2048]{1,0:T(8,128)(2,1)}, u32[]{:S(2)}) copy-start(bf16[128,2048]{1,0:T(8,128)(2,1)} %param.14) | copy-start | bytes 1572868
  0.6 7.8 %copy-start.7 = (f32[16,136,1]{1,0,2:T(8,128)S(1)}, f32[16,136,1]{1,0,2:T(8,128)}, u32[]{:S(2)}) copy-start(f32[16,136,1]{1,0,2:T(8,128)} %constant.36) | copy-start | bytes 26116
  0.7 8.9 %copy-start.8 = (f32[16,136,1]{1,0,2:T(8,128)S(1)}, f32[16,136,1]{1,0,2:T(8,128)}, u32[]{:S(2)}) copy-start(f32[16,136,1]{1,0,2:T(8,128)} %constant.37) | copy-start | bytes 26116
  0.7 8.9 %copy-start.11 = (f32[136]{0:T(256)S(1)}, f32[136]{0:T(256)}, u32[]{:S(2)}) copy-start(f32[136]{0:T(256)} %constant.35.clone) | copy-start | bytes 1636
  2.8 115.4 %collective-permute-start.8 = (bf16[128,2048]{0,1:T(8,128)(2,1)}, bf16[128,2048]{0,1:T(8,128)(2,1)}, u32[]{:S(2)}, u32[]{:S(2)}) collective-permute-start(bf16[128,2048]{0,1:T(8,128)(2,1)} %copy.67), channel_id=1, source_target_pairs={{0,8},{4,12},{8,16},{12,20},{16,24},{20,28},{1,9},{5,13},{9,17},{1... | collective-permute-start | bytes 1572872 | tf_op jit(solution)/shard_map/ppermute | solution.py:18
  4.1 114.2 %collective-permute-start.9 = (bf16[128,2048]{0,1:T(8,128)(2,1)}, bf16[128,2048]{0,1:T(8,128)(2,1)}, u32[]{:S(2)}, u32[]{:S(2)}) collective-permute-start(bf16[128,2048]{0,1:T(8,128)(2,1)} %copy.67), channel_id=1, source_target_pairs={{0,4},{4,8},{8,12},{12,16},{16,20},{20,24},{24,28},{1,5},{5,9},{9,... | collective-permute-start | bytes 1572872 | tf_op jit(solution)/shard_map/ppermute | solution.py:18
  9.5 3.9 %copy-start.1 = (bf16[128,2048]{1,0:T(8,128)(2,1)S(1)}, bf16[128,2048]{1,0:T(8,128)(2,1)}, u32[]{:S(2)}) copy-start(bf16[128,2048]{1,0:T(8,128)(2,1)} %param.13) | copy-start | bytes 1572868
  11.5 20.7 %collective-permute-start.3 = (f32[16,153]{1,0:T(8,128)S(1)}, f32[16,153]{1,0:T(8,128)S(1)}, u32[]{:S(2)}, u32[]{:S(2)}) collective-permute-start(f32[16,153]{1,0:T(8,128)S(1)} %fusion.17), channel_id=1, source_target_pairs={{0,4},{4,8},{8,12},{12,16},{16,20},{20,24},{24,28},{1,5},{5,9},{9,... | collective-permute-start | bytes 29384 | tf_op jit(solution)/shard_map/ppermute | solution.py:18
  13.4 66.6 %collective-permute-start.6 = (bf16[128,2048]{1,0:T(8,128)(2,1)S(1)}, bf16[128,2048]{1,0:T(8,128)(2,1)}, u32[]{:S(2)}, u32[]{:S(2)}) collective-permute-start(bf16[128,2048]{1,0:T(8,128)(2,1)S(1)} %copy-done.1), channel_id=1, source_target_pairs={{0,8},{4,12},{8,16},{12,20},{16,24},{20,28},{1,9},{5,13},{9,17},{1... | collective-permute-start | bytes 1572872 | tf_op jit(solution)/shard_map/ppermute | solution.py:18
  15.6 3.7 %copy-start.9 = (bf16[128,256]{1,0:T(8,128)(2,1)S(1)}, bf16[128,256]{1,0:T(8,128)(2,1)}, u32[]{:S(2)}) copy-start(bf16[128,256]{1,0:T(8,128)(2,1)} %param.11) | copy-start | bytes 196612
  17.4 52.0 %collective-permute-start = (f32[16,153,128]{2,0,1:T(8,128)}, f32[16,153,128]{2,0,1:T(8,128)}, u32[]{:S(2)}, u32[]{:S(2)}) collective-permute-start(f32[16,153,128]{2,0,1:T(8,128)} %copy.63), channel_id=1, source_target_pairs={{0,4},{4,8},{8,12},{12,16},{16,20},{20,24},{24,28},{1,5},{5,9},{9,... | collective-permute-start | bytes 3760136 | tf_op jit(solution)/shard_map/ppermute | solution.py:18
  23.5 55.2 %copy-start.4 = (f32[16,136,128]{2,1,0:T(8,128)}, f32[16,136,128]{2,1,0:T(8,128)S(1)}, u32[]{:S(2)}) copy-start(f32[16,136,128]{2,1,0:T(8,128)S(1)} %fusion.9) | copy-start | bytes 3342340
  32.2 5.6 %collective-permute-start.4 = (f32[16,153]{1,0:T(8,128)S(1)}, f32[16,153]{1,0:T(8,128)S(1)}, u32[]{:S(2)}, u32[]{:S(2)}) collective-permute-start(f32[16,153]{1,0:T(8,128)S(1)} %add.76), channel_id=1, source_target_pairs={{0,8},{4,12},{8,16},{12,20},{16,24},{20,28},{1,9},{5,13},{9,17},{1... | collective-permute-start | bytes 29384 | tf_op jit(solution)/shard_map/ppermute | solution.py:18
  37.8 36.9 %collective-permute-start.5 = (f32[16,153]{1,0:T(8,128)S(1)}, f32[16,153]{1,0:T(8,128)S(1)}, u32[]{:S(2)}, u32[]{:S(2)}) collective-permute-start(f32[16,153]{1,0:T(8,128)S(1)} %add.77), channel_id=1, source_target_pairs={{0,16},{4,20},{8,24},{12,28},{1,17},{5,21},{9,25},{13,29},{2,18},{... | collective-permute-start | bytes 29384 | tf_op jit(solution)/shard_map/ppermute | solution.py:18
  72.5 43.0 %copy-start.2 = (bf16[128,2048]{1,0:T(8,128)(2,1)S(1)}, bf16[128,2048]{1,0:T(8,128)(2,1)}, u32[]{:S(2)}) copy-start(bf16[128,2048]{1,0:T(8,128)(2,1)} %param.13) | copy-start | bytes 1572868
  72.5 47.3 %collective-permute-start.1 = (f32[16,153,128]{2,0,1:T(8,128)}, f32[16,153,128]{2,0,1:T(8,128)}, u32[]{:S(2)}, u32[]{:S(2)}) collective-permute-start(f32[16,153,128]{2,0,1:T(8,128)} %copy_add_fusion), channel_id=1, source_target_pairs={{0,8},{4,12},{8,16},{12,20},{16,24},{20,28},{1,9},{5,13},{9,17},{1... | collective-permute-start | bytes 3760136 | tf_op jit(solution)/shard_map/ppermute | solution.py:18
  74.7 40.8 %collective-permute-start.7 = (bf16[128,2048]{1,0:T(8,128)(2,1)S(1)}, bf16[128,2048]{1,0:T(8,128)(2,1)S(1)}, u32[]{:S(2)}, u32[]{:S(2)}) collective-permute-start(bf16[128,2048]{1,0:T(8,128)(2,1)S(1)} %copy-done.1), channel_id=1, source_target_pairs={{0,4},{4,8},{8,12},{12,16},{16,20},{20,24},{24,28},{1,5},{5,9},{9,... | collective-permute-start | bytes 1572872 | tf_op jit(solution)/shard_map/ppermute | solution.py:18
  121.6 57.0 %collective-permute-start.2 = (f32[16,153,128]{2,0,1:T(8,128)S(1)}, f32[16,153,128]{2,0,1:T(8,128)}, u32[]{:S(2)}, u32[]{:S(2)}) collective-permute-start(f32[16,153,128]{2,0,1:T(8,128)S(1)} %add.73), channel_id=1, source_target_pairs={{0,16},{4,20},{8,24},{12,28},{1,17},{5,21},{9,25},{13,29},{2,18},{... | collective-permute-start | bytes 3760136 | tf_op jit(solution)/shard_map/ppermute | solution.py:18
  122.9 0.8 copy-start.10
  123.7 1.4 copy-start.3
  128.6 52.1 %copy-start.5 = (f32[16,136,128]{2,1,0:T(8,128)S(1)}, f32[16,136,128]{2,1,0:T(8,128)}, u32[]{:S(2)}) copy-start(f32[16,136,128]{2,1,0:T(8,128)} %copy-done.4) | copy-start | bytes 3342340
  128.6 52.1 %copy-start.6 = (f32[128,16,128]{0,2,1:T(8,128)S(1)}, f32[128,16,128]{0,2,1:T(8,128)}, u32[]{:S(2)}) copy-start(f32[128,16,128]{0,2,1:T(8,128)} %convolution_bitcast_fusion.1) | copy-start | bytes 3145732
where the time goes:
time: 186 us
  waiting for transfers between devices  127 us (68%)
  starting transfers between devices  19.1 us (10%)
  matrix products  15.8 us (8%)
  other arithmetic  13.1 us (7%)
  local copies, waits for them, and re-layouts  9.66 us (5%)
    ppermute x10, waiting for transfers between devices, passed_along(): return lax.ppermute(block, axis, route)  127 us
    ppermute x10, starting transfers between devices, passed_along(): return lax.ppermute(block, axis, route)  19.1 us
    unnamed x27, local copies, waits for them, and re-layouts  6.12 us
    add x2, other arithmetic, on_device(): running_state = running_state + arrived[0]  4.92 us
  transfers between devices with their start and end apart: 10, of which 5 were waited for; matrix products, arithmetic and copies ran while one was open for 15% of the time, Pallas kernels for 0%

commit v1 on v0

v1 whole, which is shorter than its diff:
```python
import functools
import jax
import jax.numpy as jnp
import numpy as np
from jax import lax
from jax.experimental import pallas as pl
from jax.experimental.pallas import tpu as pltpu
from jax.sharding import PartitionSpec as P

FEAT = 16
WINDOW = 256
PAIRS = FEAT * (FEAT + 1) // 2
FEATS = 160
ONE_ROW = PAIRS + FEAT
CHUNKS = 4
MESH = pl.DeviceIdType.MESH
F32 = jnp.float32
BF16 = jnp.bfloat16


def selections(lanes):
    lower, upper = np.triu_indices(FEAT)
    left = np.zeros((FEATS, FEAT), np.float32)
    right = np.zeros((FEATS, FEAT), np.float32)
    right_query = np.zeros((FEATS, FEAT), np.float32)
    rows = np.arange(PAIRS)
    left[rows, lower] = 1.0
    right[rows, upper] = 1.0
    right_query[rows, upper] = np.where(lower == upper, 1.0, 2.0)
    left[PAIRS + np.arange(FEAT), np.arange(FEAT)] = 1.0
    stacked = np.stack([left, right, right_query])
    return jnp.asarray(np.tile(stacked, (1, 1, lanes // FEAT)), BF16)


def dot_t(a, b):
    return lax.dot_general(a, b, (((1,), (1,)), ((), ())), preferred_element_type=F32)


def dot(a, b):
    return jnp.dot(a, b, preferred_element_type=F32)


def kernel(
    pairs, rows, dim, heads,
    lq_ref, lk_ref, v_ref, wq_ref, wk_ref, sel_ref,
    lin_ref, win_ref,
    lq2, lk2, v2, q2, k2, pv, pk, num, den, state, norm, state_in, norm_in, state_out, norm_out,
    lin_f, lin_b, win_b, lin_in, win_in,
    xs, xr, zs, zr, ys, yr, cs, cr, rs, rr,
):
    me = lax.axis_index("seq")
    pair = me // 2
    par = me % 2
    other = 1 - par
    partner = {"seq": pair * 2 + other}
    ahead = {"seq": jnp.minimum(me + 2, 2 * pairs - 1)}
    behind = {"seq": jnp.maximum(me - 2, 0)}
    has_next = pair < pairs - 1
    has_prev = pair > 0
    half_heads = heads // 2
    half = half_heads * dim
    width = half // CHUNKS
    per = width // dim
    lanes = half_heads * FEAT
    mine = pl.ds(pl.multiple_of(par * rows, rows), rows)
    theirs = pl.ds(pl.multiple_of(other * rows, rows), rows)

    def own_cols(c):
        return pl.ds(pl.multiple_of(par * half + c * width, width), width)

    def other_cols(c):
        return pl.ds(pl.multiple_of(other * half + c * width, width), width)

    def cols(c):
        return pl.ds(c * width if isinstance(c, int) else pl.multiple_of(c * width, width), width)

    barrier = pltpu.get_barrier_semaphore()
    pl.semaphore_signal(barrier, inc=1, device_id=partner, device_id_type=MESH)

    @pl.when(has_next)
    def _():
        pl.semaphore_signal(barrier, inc=1, device_id=ahead, device_id_type=MESH)

    @pl.when(has_prev)
    def _():
        pl.semaphore_signal(barrier, inc=1, device_id=behind, device_id_type=MESH)

    pl.semaphore_wait(barrier, 1 + jnp.minimum(pair, 1) + jnp.minimum(pairs - 1 - pair, 1))

    def remote(src, dst, send, recv, where):
        return pltpu.make_async_remote_copy(
            src_ref=src, dst_ref=dst, send_sem=send, recv_sem=recv,
            device_id=where, device_id_type=MESH,
        )

    small_other = pl.ds(pl.multiple_of(other * lanes, lanes), lanes)
    small_own = pl.ds(pl.multiple_of(par * lanes, lanes), lanes)

    def x_lk():
        return remote(lk_ref.at[:, small_other], lk2.at[mine, :], xs.at[0], xr.at[0], partner)

    def x_lq():
        return remote(lq_ref.at[:, small_other], lq2.at[mine, :], xs.at[1], xr.at[1], partner)

    def x_copy(src, dst, slot, c):
        at = 2 + slot * CHUNKS + c
        return remote(src.at[:, other_cols(c)], dst.at[mine, cols(c)], xs.at[at], xr.at[at], partner)

    def x_v(c):
        return x_copy(v_ref, v2, 0, c)

    def x_k(c):
        return x_copy(wk_ref, k2, 1, c)

    def x_q(c):
        return x_copy(wq_ref, q2, 2, c)

    def z_v(c):
        return remote(v_ref.at[:, own_cols(c)], pv.at[mine, cols(c)], zs.at[c], zr.at[c], ahead)

    def z_k(c):
        at = CHUNKS + c
        return remote(wk_ref.at[:, own_cols(c)], pk.at[mine, cols(c)], zs.at[at], zr.at[at], ahead)

    def y_v(c):
        return remote(v2.at[theirs, cols(c)], pv.at[theirs, cols(c)], ys.at[c], yr.at[c], ahead)

    def y_k(c):
        at = CHUNKS + c
        return remote(k2.at[theirs, cols(c)], pk.at[theirs, cols(c)], ys.at[at], yr.at[at], ahead)

    def c_state(c):
        return remote(state_out.at[c], state_in.at[c], cs.at[c], cr.at[c], ahead)

    def c_norm():
        return remote(norm_out, norm_in, cs.at[CHUNKS], cr.at[CHUNKS], ahead)

    def r_lin(c):
        return remote(lin_b.at[theirs, cols(c)], lin_in.at[:, cols(c)], rs.at[c], rr.at[c], partner)

    def r_win(c):
        at = CHUNKS + c
        return remote(win_b.at[theirs, cols(c)], win_in.at[:, cols(c)], rs.at[at], rr.at[at], partner)

    x_lk().start()
    x_lq().start()
    for c in range(CHUNKS):
        x_v(c).start()
        x_k(c).start()

        @pl.when(has_next)
        def _():
            z_v(c).start()
            z_k(c).start()

    for c in range(CHUNKS):
        x_q(c).start()

    lq2[mine, :] = lq_ref[:, small_own]
    lk2[mine, :] = lk_ref[:, small_own]
    for c in range(CHUNKS):
        v2[mine, cols(c)] = v_ref[:, own_cols(c)]
        k2[mine, cols(c)] = wk_ref[:, own_cols(c)]
        q2[mine, cols(c)] = wq_ref[:, own_cols(c)]

    @pl.when(pair == 0)
    def _():
        pv[...] = jnp.zeros_like(pv)
        pk[...] = jnp.zeros_like(pk)
        state_in[...] = jnp.zeros_like(state_in)
        norm_in[...] = jnp.zeros_like(norm_in)

    norm[...] = jnp.zeros_like(norm)
    x_lk().wait_recv()
    x_lq().wait_recv()

    both = 2 * rows
    ones = jnp.ones((both, dim), BF16)
    lane = lax.broadcasted_iota(jnp.int32, (both, lanes), 1) // FEAT
    row_at = lax.broadcasted_iota(jnp.int32, (both, both), 0)
    col_at = lax.broadcasted_iota(jnp.int32, (both, both), 1)
    causal = col_at <= row_at
    feat_row = lax.broadcasted_iota(jnp.int32, (FEATS, both), 0)
    row_left = jnp.where(feat_row == ONE_ROW, 1.0, 0.0)
    row_right = jnp.where((feat_row >= PAIRS) & (feat_row <= ONE_ROW), 1.0, 0.0)
    norm_lane = lax.broadcasted_iota(jnp.int32, (FEATS, 128), 1)

    def first(c, carry):
        x_v(c).wait_recv()
        x_k(c).wait_recv()

        @pl.when(has_next)
        def _():
            y_v(c).start()
            y_k(c).start()

        for u in range(per):
            head = c * per + u
            at = pl.ds(pl.multiple_of(head * dim, dim), dim)
            chosen = lane == head
            keys = lk2[...]
            key_m = jnp.where(chosen, keys.astype(F32), 0.0).astype(BF16)
            query_m = jnp.where(chosen, lq2[...].astype(F32) * 0.25, 0.0).astype(BF16)
            values = jnp.concatenate([v2[:, at], ones], axis=1)
            feats = (dot_t(sel_ref[0], key_m) + row_left) * (dot_t(sel_ref[1], key_m) + row_right)
            summed = dot(feats.astype(BF16), values)
            state[head] = summed[:, :dim]
            norm[...] += jnp.where(norm_lane == head, summed[:, dim:], 0.0)
            a = dot_t(query_m, keys) + 1.0
            weight = jnp.where(causal, a * a + 1.0, 0.0).astype(BF16)
            mixed = dot(weight, values)
            num[:, at] = mixed[:, :dim]
            den[:, at] = mixed[:, dim:]
        return carry

    lax.fori_loop(0, CHUNKS, first, 0)

    @pl.when(has_prev)
    def _():
        c_norm().wait_recv()

    @pl.when(has_next)
    def _():
        norm_out[...] = norm_in[...] + norm[...]
        c_norm().start()

    def chain(c, carry):
        @pl.when(has_prev)
        def _():
            c_state(c).wait_recv()

        @pl.when(has_next)
        def _():
            total = state_in[c].astype(F32) + state[pl.ds(c * per, per)]
            state_out[c] = total.astype(state_out.dtype)
            c_state(c).start()

        return carry

    lax.fori_loop(0, CHUNKS, chain, 0)

    span = 3 * rows
    q_at = lax.broadcasted_iota(jnp.int32, (rows, span), 0)
    k_at = lax.broadcasted_iota(jnp.int32, (rows, span), 1)
    band = (k_at > q_at) & (k_at <= q_at + both)
    empty = jnp.where(pair == 0, 1, 0)
    factor = dim ** -0.5 * 1.4426950408889634
    feat_lane = lax.broadcasted_iota(jnp.int32, (both, FEATS), 1)
    lane_left = jnp.where(feat_lane == ONE_ROW, 1.0, 0.0)
    lane_right = jnp.where((feat_lane >= PAIRS) & (feat_lane <= ONE_ROW), 2.0, 0.0)
    wide_ones = jnp.ones((span, dim), BF16)

    def second(c, carry):
        x_q(c).wait_recv()

        @pl.when(has_prev)
        def _():
            z_v(c).wait_recv()
            z_k(c).wait_recv()
            y_v(c).wait_recv()
            y_k(c).wait_recv()

        for u in range(per):
            head = c * per + u
            at = pl.ds(pl.multiple_of(head * dim, dim), dim)
            for part in range(2):
                begin = part * rows
                keys = jnp.concatenate([pk[begin:, at], k2[: begin + rows, at]], axis=0)
                values = jnp.concatenate([pv[begin:, at], v2[: begin + rows, at]], axis=0)
                scores = dot_t(q2[begin : begin + rows, at], keys) * factor
                allowed = band & (k_at >= empty * (both - begin))
                scores = jnp.where(allowed, scores, -1e30)
                largest = jnp.max(scores, axis=1, keepdims=True)
                weight = jnp.exp2(scores - largest).astype(BF16)
                mixed = dot(weight, jnp.concatenate([values, wide_ones], axis=1))
                win_b[begin : begin + rows, at] = (mixed[:, :dim] / mixed[:, dim:]).astype(BF16)

            query_m = jnp.where(lane == head, lq2[...].astype(F32) * 0.25, 0.0).astype(BF16)
            feats = (dot_t(query_m, sel_ref[0]) + lane_left) * (dot_t(query_m, sel_ref[2]) + lane_right)
            norm_col = jnp.sum(jnp.where(norm_lane == head, norm_in[...], 0.0), axis=1, keepdims=True)
            prior = jnp.concatenate(
                [state_in[c, u].astype(BF16), jnp.broadcast_to(norm_col, (FEATS, dim)).astype(BF16)], axis=1
            )
            added = dot(feats.astype(BF16), prior)
            linear = (num[:, at] + added[:, :dim]) / (den[:, at] + added[:, dim:])
            lin_f[:, at] = linear
            lin_b[:, at] = linear.astype(BF16)
        r_lin(c).start()
        r_win(c).start()
        win_ref[:, own_cols(c)] = win_b[mine, cols(c)]
        lin_ref[:, own_cols(c)] = lin_f[mine, cols(c)]
        return carry

    lax.fori_loop(0, CHUNKS, second, 0)

    def last(c, carry):
        r_lin(c).wait_recv()
        r_win(c).wait_recv()
        win_ref[:, other_cols(c)] = win_in[:, cols(c)]
        lin_ref[:, other_cols(c)] = lin_in[:, cols(c)].astype(F32)
        return carry

    lax.fori_loop(0, CHUNKS, last, 0)

    x_lk().wait_send()
    x_lq().wait_send()
    for c in range(CHUNKS):
        x_v(c).wait_send()
        x_k(c).wait_send()
        x_q(c).wait_send()
        r_lin(c).wait_send()
        r_win(c).wait_send()

    @pl.when(has_next)
    def _():
        c_norm().wait_send()
        for c in range(CHUNKS):
            z_v(c).wait_send()
            z_k(c).wait_send()
            y_v(c).wait_send()
            y_k(c).wait_send()
            c_state(c).wait_send()


def on_device(linear_query, linear_key, values, window_query, window_key):
    rows, width = values.shape
    heads = linear_query.shape[1] // FEAT
    dim = width // heads
    pairs = lax.axis_size("seq") // 2
    half_heads = heads // 2
    half = width // 2
    lanes = half_heads * FEAT
    both = 2 * rows
    per = half_heads // CHUNKS
    state_type = BF16 if pairs <= 8 else F32
    vmem = pl.BlockSpec(memory_space=pltpu.VMEM)
    dma = pltpu.SemaphoreType.DMA
    return pl.pallas_call(
        functools.partial(kernel, pairs, rows, dim, heads),
        out_shape=(
            jax.ShapeDtypeStruct((rows, width), F32),
            jax.ShapeDtypeStruct((rows, width), BF16),
        ),
        in_specs=[vmem] * 6,
        out_specs=(vmem, vmem),
        scratch_shapes=[
            pltpu.VMEM((both, lanes), BF16),
            pltpu.VMEM((both, lanes), BF16),
            pltpu.VMEM((both, half), BF16),
            pltpu.VMEM((both, half), BF16),
            pltpu.VMEM((both, half), BF16),
            pltpu.VMEM((both, half), BF16),
            pltpu.VMEM((both, half), BF16),
            pltpu.VMEM((both, half), F32),
            pltpu.VMEM((both, half), F32),
            pltpu.VMEM((half_heads, FEATS, dim), F32),
            pltpu.VMEM((FEATS, 128), F32),
            pltpu.VMEM((CHUNKS, per, FEATS, dim), state_type),
            pltpu.VMEM((FEATS, 128), F32),
            pltpu.VMEM((CHUNKS, per, FEATS, dim), state_type),
            pltpu.VMEM((FEATS, 128), F32),
            pltpu.VMEM((both, half), F32),
            pltpu.VMEM((both, half), BF16),
            pltpu.VMEM((both, half), BF16),
            pltpu.VMEM((rows, half), BF16),
            pltpu.VMEM((rows, half), BF16),
            dma((2 + 3 * CHUNKS,)),
            dma((2 + 3 * CHUNKS,)),
            dma((2 * CHUNKS,)),
            dma((2 * CHUNKS,)),
            dma((2 * CHUNKS,)),
            dma((2 * CHUNKS,)),
            dma((CHUNKS + 1,)),
            dma((CHUNKS + 1,)),
            dma((2 * CHUNKS,)),
            dma((2 * CHUNKS,)),
        ],
        compiler_params=pltpu.CompilerParams(
            collective_id=0, has_side_effects=True, vmem_limit_bytes=48 * 1024 * 1024
        ),
        cost_estimate=pl.CostEstimate(
            flops=4_000_000_000, bytes_accessed=4_000_000, transcendentals=1_600_000
        ),
    )(linear_query, linear_key, values, window_query, window_key, selections(lanes))


def solution(mesh):
    spec = P(("grp", "seq"), None)
    return jax.shard_map(
        on_device,
        mesh=mesh,
        in_specs=(spec,) * 5,
        out_specs=(spec, spec),
        check_vma=False,
    )
```

time: 186 us -> 62.8 us (0.34)
  waiting for transfers between devices: 127 us -> 0 us
  Pallas kernels: 0 us -> 54.3 us
  starting transfers between devices: 19.1 us -> 0 us
  matrix products: 15.8 us -> 0 us
  other arithmetic: 13.1 us -> 0 us
  local copies, waits for them, and re-layouts: 9.66 us -> 7.46 us
    ppermute x10 -> x0, waiting for transfers between devices: 127 us -> none  [passed_along(): return lax.ppermute(block, axis, route)]
    pallas_call x0 -> x1, Pallas kernels: none -> 54.3 us  [on_device(): pl.pallas_call(functools.partial(kernel, pairs, rows, dim, heads), out_sh...]
    ppermute x10 -> x0, starting transfers between devices: 19.1 us -> none  [passed_along(): return lax.ppermute(block, axis, route)]
    dot_general x11 -> x0, matrix products: 15.8 us -> none  [the longest x1 3.69 us: on_device(): jnp.einsum('hpt,hpv->thv', query_feats, prior_state, precision=PRECISE)]
    add x7 -> x0, other arithmetic: 4.94 us -> none  [the longest x2 4.92 us: on_device(): running_state = running_state + arrived[0]]
    sub x3 -> x0, other arithmetic: 3.01 us -> none  [the longest x1 2.07 us: on_device(): prior_state = running_state - local_state]
    concatenate x2 -> x0, other arithmetic: 2.71 us -> none  [the longest x1 1.57 us: on_device(): all_keys = jnp.concatenate(moved_keys[::-1] + [window_key], axis=0)]
    unnamed x27 -> x14, local copies, waits for them, and re-layouts: 6.12 us -> 7.46 us
  transfers between devices with their start and end apart: 10 -> 0, of which waited for: 5 -> 0; matrix products, arithmetic and copies ran while one was open for 15% -> 0% of each run, Pallas kernels for 0% -> 0%
where the time goes in v1:
time: 62.8 us; the launch traced here: 62.4 us
  Pallas kernels  54.3 us (86%)
  local copies, waits for them, and re-layouts  7.46 us (12%)
  between operations  0.65 us (1%)
    pallas_call x1, Pallas kernels, on_device(): pl.pallas_call(functools.partial(kernel, pairs, rows, dim, heads), out_sh...  54.3 us
    unnamed x14, local copies, waits for them, and re-layouts  7.46 us

profile of v1, /device:TPU:24, one launch (start us, length us, event | category | flops | bytes accessed | tf_op | source)
XLA Modules:
  0.0 62.4 jit_solution(2971190286585862430)
XLA Ops:
  0.6 0.0 copy-start
  0.6 1.0 %copy-done = bf16[128,2048]{1,0:T(8,128)(2,1)S(1)} copy-done((bf16[128,2048]{1,0:T(8,128)(2,1)S(1)}, bf16[128,2048]{1,0:T(8,128)(2,1)}, u32[]{:S(2)}) %copy-start) | copy-done | bytes 524312
  1.7 0.0 copy-start.1
  1.7 1.0 %copy-done.1 = bf16[128,2048]{1,0:T(8,128)(2,1)S(1)} copy-done((bf16[128,2048]{1,0:T(8,128)(2,1)S(1)}, bf16[128,2048]{1,0:T(8,128)(2,1)}, u32[]{:S(2)}) %copy-start.1) | copy-done | bytes 524312
  2.7 0.0 copy-start.2
  2.7 1.0 %copy-done.2 = bf16[128,2048]{1,0:T(8,128)(2,1)S(1)} copy-done((bf16[128,2048]{1,0:T(8,128)(2,1)S(1)}, bf16[128,2048]{1,0:T(8,128)(2,1)}, u32[]{:S(2)}) %copy-start.2) | copy-done | bytes 524312
  3.8 0.0 copy-start.3
  3.8 0.8 %copy-done.3 = bf16[128,256]{1,0:T(8,128)(2,1)S(1)} copy-done((bf16[128,256]{1,0:T(8,128)(2,1)S(1)}, bf16[128,256]{1,0:T(8,128)(2,1)}, u32[]{:S(2)}) %copy-start.3) | copy-done | bytes 65560
  4.6 0.0 copy-start.4
  4.6 0.8 %copy-done.4 = bf16[128,256]{1,0:T(8,128)(2,1)S(1)} copy-done((bf16[128,256]{1,0:T(8,128)(2,1)S(1)}, bf16[128,256]{1,0:T(8,128)(2,1)}, u32[]{:S(2)}) %copy-start.4) | copy-done | bytes 65560
  5.4 0.0 copy-start.5
  5.4 0.9 %copy-done.5 = bf16[3,160,128]{2,1,0:T(8,128)(2,1)S(1)} copy-done((bf16[3,160,128]{2,1,0:T(8,128)(2,1)S(1)}, bf16[3,160,128]{2,1,0:T(8,128)(2,1)}, u32[]{:S(2)}) %copy-start.5) | copy-done | bytes 122904
  6.3 54.3 %shard_map.77 = (f32[128,2048]{1,0:T(8,128)S(1)}, bf16[128,2048]{1,0:T(8,128)(2,1)S(1)}) custom-call(bf16[128,256]{1,0:T(8,128)(2,1)S(1)} %copy-done.3, bf16[128,256]{1,0:T(8,128)(2,1)S(1)} %copy-done.4, bf16[128,2048]{1,0:T(8,128)(2,1)S(1)} %copy-done, bf16[128,2048]{1,0:T(8,128)(2,1)S(1)} %copy-done.1, bf16[128,2048]{1,0:T(8,128)(2,1)S(1)} %copy-done.2, ...), custom_call_target="tpu_custom_call" | custom-call | flops 4000000000 | bytes 4000000 | tf_op jit(solution)/shard_map/pallas_call | solution.py:338
  60.7 1.0 %copy.10 = f32[128,2048]{1,0:T(8,128)} copy(f32[128,2048]{1,0:T(8,128)S(1)} %get-tuple-element.4) | data formatting | bytes 2097152
  61.7 0.8 %copy.11 = bf16[128,2048]{1,0:T(8,128)(2,1)} copy(bf16[128,2048]{1,0:T(8,128)(2,1)S(1)} %get-tuple-element.5) | data formatting | bytes 1048576
Async XLA Ops:
  0.6 1.0 %copy-start = (bf16[128,2048]{1,0:T(8,128)(2,1)S(1)}, bf16[128,2048]{1,0:T(8,128)(2,1)}, u32[]{:S(2)}) copy-start(bf16[128,2048]{1,0:T(8,128)(2,1)} %v_ref.1) | copy-start | bytes 1572868
  1.7 1.0 %copy-start.1 = (bf16[128,2048]{1,0:T(8,128)(2,1)S(1)}, bf16[128,2048]{1,0:T(8,128)(2,1)}, u32[]{:S(2)}) copy-start(bf16[128,2048]{1,0:T(8,128)(2,1)} %wq_ref.1) | copy-start | bytes 1572868
  2.7 1.0 %copy-start.2 = (bf16[128,2048]{1,0:T(8,128)(2,1)S(1)}, bf16[128,2048]{1,0:T(8,128)(2,1)}, u32[]{:S(2)}) copy-start(bf16[128,2048]{1,0:T(8,128)(2,1)} %wk_ref.1) | copy-start | bytes 1572868
  3.8 0.8 %copy-start.3 = (bf16[128,256]{1,0:T(8,128)(2,1)S(1)}, bf16[128,256]{1,0:T(8,128)(2,1)}, u32[]{:S(2)}) copy-start(bf16[128,256]{1,0:T(8,128)(2,1)} %lq_ref.1) | copy-start | bytes 196612
  4.6 0.8 %copy-start.4 = (bf16[128,256]{1,0:T(8,128)(2,1)S(1)}, bf16[128,256]{1,0:T(8,128)(2,1)}, u32[]{:S(2)}) copy-start(bf16[128,256]{1,0:T(8,128)(2,1)} %lk_ref.1) | copy-start | bytes 196612
  5.4 0.9 %copy-start.5 = (bf16[3,160,128]{2,1,0:T(8,128)(2,1)S(1)}, bf16[3,160,128]{2,1,0:T(8,128)(2,1)}, u32[]{:S(2)}) copy-start(bf16[3,160,128]{2,1,0:T(8,128)(2,1)} %constant.2.clone.sel_ref) | copy-start | bytes 368644

commit v2 on v1

--- a/solution.py
+++ b/solution.py
@@ -42,11 +42,11 @@
 
 def kernel(
     pairs, rows, dim, heads,
-    lq_ref, lk_ref, v_ref, wq_ref, wk_ref, sel_ref,
+    lq_ref, lk_ref, v_ref, wq_ref, wk_ref, sel_in,
     lin_ref, win_ref,
-    lq2, lk2, v2, q2, k2, pv, pk, num, den, state, norm, state_in, norm_in, state_out, norm_out,
+    sel_ref, lq2, lk2, v2, q2, k2, pv, pk, num, den, state, norm, state_in, norm_in, state_out, norm_out,
     lin_f, lin_b, win_b, lin_in, win_in,
-    xs, xr, zs, zr, ys, yr, cs, cr, rs, rr,
+    xs, xr, zs, zr, ys, yr, cs, cr, rs, rr, ls,
 ):
     me = lax.axis_index("seq")
     pair = me // 2
@@ -142,26 +142,43 @@
         at = CHUNKS + c
         return remote(win_b.at[theirs, cols(c)], win_in.at[:, cols(c)], rs.at[at], rr.at[at], partner)
 
+    def local(src, dst, at):
+        return pltpu.make_async_copy(src, dst, ls.at[at])
+
+    def z_own(c):
+        z_v(c).start()
+        z_k(c).start()
+
     x_lk().start()
     x_lq().start()
     for c in range(CHUNKS):
         x_v(c).start()
+
+    @pl.when(has_next)
+    def _():
+        z_own(0)
+
+        @pl.when(has_prev)
+        def _():
+            z_own(1)
+
+    small = [
+        local(sel_in, sel_ref, 0),
+        local(lk_ref.at[:, small_own], lk2.at[mine, :], 1),
+        local(lq_ref.at[:, small_own], lq2.at[mine, :], 2),
+    ]
+    all_own = pl.ds(pl.multiple_of(par * half, half), half)
+    large = [
+        local(v_ref.at[:, all_own], v2.at[mine, :], 3),
+        local(wk_ref.at[:, all_own], k2.at[mine, :], 4),
+        local(wq_ref.at[:, all_own], q2.at[mine, :], 5),
+    ]
+    for copy in small + large:
+        copy.start()
+    for c in range(CHUNKS):
         x_k(c).start()
-
-        @pl.when(has_next)
-        def _():
-            z_v(c).start()
-            z_k(c).start()
-
     for c in range(CHUNKS):
         x_q(c).start()
-
-    lq2[mine, :] = lq_ref[:, small_own]
-    lk2[mine, :] = lk_ref[:, small_own]
-    for c in range(CHUNKS):
-        v2[mine, cols(c)] = v_ref[:, own_cols(c)]
-        k2[mine, cols(c)] = wk_ref[:, own_cols(c)]
-        q2[mine, cols(c)] = wq_ref[:, own_cols(c)]
 
     @pl.when(pair == 0)
     def _():
@@ -171,6 +188,8 @@
         norm_in[...] = jnp.zeros_like(norm_in)
 
     norm[...] = jnp.zeros_like(norm)
+    for copy in small + large:
+        copy.wait()
     x_lk().wait_recv()
     x_lq().wait_recv()
 
@@ -187,13 +206,6 @@
 
     def first(c, carry):
         x_v(c).wait_recv()
-        x_k(c).wait_recv()
-
-        @pl.when(has_next)
-        def _():
-            y_v(c).start()
-            y_k(c).start()
-
         for u in range(per):
             head = c * per + u
             at = pl.ds(pl.multiple_of(head * dim, dim), dim)
@@ -211,20 +223,7 @@
             mixed = dot(weight, values)
             num[:, at] = mixed[:, :dim]
             den[:, at] = mixed[:, dim:]
-        return carry
-
-    lax.fori_loop(0, CHUNKS, first, 0)
-
-    @pl.when(has_prev)
-    def _():
-        c_norm().wait_recv()
-
-    @pl.when(has_next)
-    def _():
-        norm_out[...] = norm_in[...] + norm[...]
-        c_norm().start()
-
-    def chain(c, carry):
+
         @pl.when(has_prev)
         def _():
             c_state(c).wait_recv()
@@ -237,7 +236,39 @@
 
         return carry
 
-    lax.fori_loop(0, CHUNKS, chain, 0)
+    lax.fori_loop(0, CHUNKS, first, 0)
+
+    @pl.when(has_prev)
+    def _():
+        c_norm().wait_recv()
+
+    @pl.when(has_next)
+    def _():
+        norm_out[...] = norm_in[...] + norm[...]
+        c_norm().start()
+
+    def relay(c):
+        x_k(c).wait_recv()
+
+        @pl.when(has_next)
+        def _():
+            y_v(c).start()
+            y_k(c).start()
+
+    relay(0)
+
+    @pl.when(has_next & (pair == 0))
+    def _():
+        z_own(1)
+
+    relay(1)
+    for c in range(2, CHUNKS):
+
+        @pl.when(has_next)
+        def _():
+            z_own(c)
+
+        relay(c)
 
     span = 3 * rows
     q_at = lax.broadcasted_iota(jnp.int32, (rows, span), 0)
@@ -341,9 +372,10 @@
             jax.ShapeDtypeStruct((rows, width), F32),
             jax.ShapeDtypeStruct((rows, width), BF16),
         ),
-        in_specs=[vmem] * 6,
+        in_specs=[pl.BlockSpec(memory_space=pl.ANY)] * 6,
         out_specs=(vmem, vmem),
         scratch_shapes=[
+            pltpu.VMEM((3, FEATS, lanes), BF16),
             pltpu.VMEM((both, lanes), BF16),
             pltpu.VMEM((both, lanes), BF16),
             pltpu.VMEM((both, half), BF16),
@@ -374,9 +406,10 @@
             dma((CHUNKS + 1,)),
             dma((2 * CHUNKS,)),
             dma((2 * CHUNKS,)),
+            dma((6,)),
         ],
         compiler_params=pltpu.CompilerParams(
-            collective_id=0, has_side_effects=True, vmem_limit_bytes=48 * 1024 * 1024
+            collective_id=0, has_side_effects=True, vmem_limit_bytes=60 * 1024 * 1024
         ),
         cost_estimate=pl.CostEstimate(
             flops=4_000_000_000, bytes_accessed=4_000_000, transcendentals=1_600_000

time: 62.8 us -> 50.9 us (0.81)
  Pallas kernels: 54.3 us -> 47 us
  local copies, waits for them, and re-layouts: 7.46 us -> 3.15 us
    pallas_call x1, Pallas kernels: 54.3 us -> 47 us  [on_device(): pl.pallas_call(functools.partial(kernel, pairs, rows, dim, heads), out_sh...]
    unnamed x14 -> x4, local copies, waits for them, and re-layouts: 7.46 us -> 3.15 us
where the time goes in v2:
time: 50.9 us; the launch traced here: 50.8 us
  Pallas kernels  47 us (92%)
  local copies, waits for them, and re-layouts  3.15 us (6%)
  between operations  0.65 us (1%)
    pallas_call x1, Pallas kernels, on_device(): pl.pallas_call(functools.partial(kernel, pairs, rows, dim, heads), out_sh...  47 us
    unnamed x4, local copies, waits for them, and re-layouts  3.15 us

profile of v2, /device:TPU:24, one launch (start us, length us, event | category | flops | bytes accessed | tf_op | source)
XLA Modules:
  0.0 50.8 jit_solution(3611613713180168723)
XLA Ops:
  0.6 47.0 %shard_map.77 = (f32[128,2048]{1,0:T(8,128)}, bf16[128,2048]{1,0:T(8,128)(2,1)}) custom-call(bf16[128,256]{1,0:T(8,128)(2,1)} %lq_ref.1, bf16[128,256]{1,0:T(8,128)(2,1)} %lk_ref.1, bf16[128,2048]{1,0:T(8,128)(2,1)} %v_ref.1, bf16[128,2048]{1,0:T(8,128)(2,1)} %wq_ref.1, bf16[128,2048]{1,0:T(8,128)(2,1)} %wk_ref.1, bf16[3,160,128]{2,1,0:T(8,128)(2,1)} %constant.2.clone.sel_in), custom_call_target="tpu_custom_call" | custom-call | flops 4000000000 | bytes 4000000 | tf_op jit(solution)/shard_map/pallas_call | solution.py:369
  47.6 0.0 copy-start
  47.6 2.4 %copy.10 = f32[128,2048]{1,0:T(8,128)} copy(f32[128,2048]{1,0:T(8,128)} %get-tuple-element.4) | data formatting | bytes 2097152
  50.0 0.0 copy-done
  50.0 0.8 %copy.11 = bf16[128,2048]{1,0:T(8,128)(2,1)} copy(bf16[128,2048]{1,0:T(8,128)(2,1)S(1)} %copy-done) | data formatting | bytes 1048576
Async XLA Ops:
  47.6 2.4 %copy-start = (bf16[128,2048]{1,0:T(8,128)(2,1)S(1)}, bf16[128,2048]{1,0:T(8,128)(2,1)}, u32[]{:S(2)}) copy-start(bf16[128,2048]{1,0:T(8,128)(2,1)} %get-tuple-element.5) | copy-start | bytes 1572868

commit v3 on v2

--- a/solution.py
+++ b/solution.py
@@ -45,7 +45,7 @@
     lq_ref, lk_ref, v_ref, wq_ref, wk_ref, sel_in,
     lin_ref, win_ref,
     sel_ref, lq2, lk2, v2, q2, k2, pv, pk, num, den, state, norm, state_in, norm_in, state_out, norm_out,
-    lin_f, lin_b, win_b, lin_in, win_in,
+    lin_b, win_b, bias,
     xs, xr, zs, zr, ys, yr, cs, cr, rs, rr, ls,
 ):
     me = lax.axis_index("seq")
@@ -136,18 +136,20 @@
         return remote(norm_out, norm_in, cs.at[CHUNKS], cr.at[CHUNKS], ahead)
 
     def r_lin(c):
-        return remote(lin_b.at[theirs, cols(c)], lin_in.at[:, cols(c)], rs.at[c], rr.at[c], partner)
+        return remote(lin_b.at[theirs, cols(c)], lin_ref.at[:, own_cols(c)], rs.at[c], rr.at[c], partner)
 
     def r_win(c):
         at = CHUNKS + c
-        return remote(win_b.at[theirs, cols(c)], win_in.at[:, cols(c)], rs.at[at], rr.at[at], partner)
+        return remote(win_b.at[theirs, cols(c)], win_ref.at[:, own_cols(c)], rs.at[at], rr.at[at], partner)
 
     def local(src, dst, at):
         return pltpu.make_async_copy(src, dst, ls.at[at])
 
-    def z_own(c):
-        z_v(c).start()
-        z_k(c).start()
+    def l_lin(c):
+        return local(lin_b.at[mine, cols(c)], lin_ref.at[:, own_cols(c)], 6 + c)
+
+    def l_win(c):
+        return local(win_b.at[mine, cols(c)], win_ref.at[:, own_cols(c)], 6 + CHUNKS + c)
 
     x_lk().start()
     x_lq().start()
@@ -156,11 +158,7 @@
 
     @pl.when(has_next)
     def _():
-        z_own(0)
-
-        @pl.when(has_prev)
-        def _():
-            z_own(1)
+        z_v(0).start()
 
     small = [
         local(sel_in, sel_ref, 0),
@@ -188,12 +186,20 @@
         norm_in[...] = jnp.zeros_like(norm_in)
 
     norm[...] = jnp.zeros_like(norm)
+    both = 2 * rows
+    span = 3 * rows
+    q_at = lax.broadcasted_iota(jnp.int32, (rows, span), 0)
+    k_at = lax.broadcasted_iota(jnp.int32, (rows, span), 1)
+    band = (k_at > q_at) & (k_at <= q_at + both)
+    empty = jnp.where(pair == 0, 1, 0)
+    for part in range(2):
+        allowed = band & (k_at >= empty * (both - part * rows))
+        bias[part] = jnp.where(allowed, 0.0, -1e30)
     for copy in small + large:
         copy.wait()
     x_lk().wait_recv()
     x_lq().wait_recv()
 
-    both = 2 * rows
     ones = jnp.ones((both, dim), BF16)
     lane = lax.broadcasted_iota(jnp.int32, (both, lanes), 1) // FEAT
     row_at = lax.broadcasted_iota(jnp.int32, (both, both), 0)
@@ -234,6 +240,10 @@
             state_out[c] = total.astype(state_out.dtype)
             c_state(c).start()
 
+        @pl.when(has_next & (c < CHUNKS - 1))
+        def _():
+            z_v(c + 1).start()
+
         return carry
 
     lax.fori_loop(0, CHUNKS, first, 0)
@@ -247,34 +257,15 @@
         norm_out[...] = norm_in[...] + norm[...]
         c_norm().start()
 
-    def relay(c):
+    for c in range(CHUNKS):
         x_k(c).wait_recv()
 
         @pl.when(has_next)
         def _():
             y_v(c).start()
+            z_k(c).start()
             y_k(c).start()
 
-    relay(0)
-
-    @pl.when(has_next & (pair == 0))
-    def _():
-        z_own(1)
-
-    relay(1)
-    for c in range(2, CHUNKS):
-
-        @pl.when(has_next)
-        def _():
-            z_own(c)
-
-        relay(c)
-
-    span = 3 * rows
-    q_at = lax.broadcasted_iota(jnp.int32, (rows, span), 0)
-    k_at = lax.broadcasted_iota(jnp.int32, (rows, span), 1)
-    band = (k_at > q_at) & (k_at <= q_at + both)
-    empty = jnp.where(pair == 0, 1, 0)
     factor = dim ** -0.5 * 1.4426950408889634
     feat_lane = lax.broadcasted_iota(jnp.int32, (both, FEATS), 1)
     lane_left = jnp.where(feat_lane == ONE_ROW, 1.0, 0.0)
@@ -298,9 +289,7 @@
                 begin = part * rows
                 keys = jnp.concatenate([pk[begin:, at], k2[: begin + rows, at]], axis=0)
                 values = jnp.concatenate([pv[begin:, at], v2[: begin + rows, at]], axis=0)
-                scores = dot_t(q2[begin : begin + rows, at], keys) * factor
-                allowed = band & (k_at >= empty * (both - begin))
-                scores = jnp.where(allowed, scores, -1e30)
+                scores = dot_t(q2[begin : begin + rows, at], keys) * factor + bias[part]
                 largest = jnp.max(scores, axis=1, keepdims=True)
                 weight = jnp.exp2(scores - largest).astype(BF16)
                 mixed = dot(weight, jnp.concatenate([values, wide_ones], axis=1))
@@ -314,12 +303,11 @@
             )
             added = dot(feats.astype(BF16), prior)
             linear = (num[:, at] + added[:, :dim]) / (den[:, at] + added[:, dim:])
-            lin_f[:, at] = linear
             lin_b[:, at] = linear.astype(BF16)
         r_lin(c).start()
         r_win(c).start()
-        win_ref[:, own_cols(c)] = win_b[mine, cols(c)]
-        lin_ref[:, own_cols(c)] = lin_f[mine, cols(c)]
+        l_lin(c).start()
+        l_win(c).start()
         return carry
 
     lax.fori_loop(0, CHUNKS, second, 0)
@@ -327,8 +315,8 @@
     def last(c, carry):
         r_lin(c).wait_recv()
         r_win(c).wait_recv()
-        win_ref[:, other_cols(c)] = win_in[:, cols(c)]
-        lin_ref[:, other_cols(c)] = lin_in[:, cols(c)].astype(F32)
+        l_lin(c).wait()
+        l_win(c).wait()
         return carry
 
     lax.fori_loop(0, CHUNKS, last, 0)
@@ -364,16 +352,15 @@
     both = 2 * rows
     per = half_heads // CHUNKS
     state_type = BF16 if pairs <= 8 else F32
-    vmem = pl.BlockSpec(memory_space=pltpu.VMEM)
     dma = pltpu.SemaphoreType.DMA
-    return pl.pallas_call(
+    linear, window = pl.pallas_call(
         functools.partial(kernel, pairs, rows, dim, heads),
         out_shape=(
-            jax.ShapeDtypeStruct((rows, width), F32),
+            jax.ShapeDtypeStruct((rows, width), BF16),
             jax.ShapeDtypeStruct((rows, width), BF16),
         ),
         in_specs=[pl.BlockSpec(memory_space=pl.ANY)] * 6,
-        out_specs=(vmem, vmem),
+        out_specs=(pl.BlockSpec(memory_space=pl.ANY),) * 2,
         scratch_shapes=[
             pltpu.VMEM((3, FEATS, lanes), BF16),
             pltpu.VMEM((both, lanes), BF16),
@@ -391,11 +378,9 @@
             pltpu.VMEM((FEATS, 128), F32),
             pltpu.VMEM((CHUNKS, per, FEATS, dim), state_type),
             pltpu.VMEM((FEATS, 128), F32),
-            pltpu.VMEM((both, half), F32),
-            pltpu.VMEM((both, half), BF16),
-            pltpu.VMEM((both, half), BF16),
-            pltpu.VMEM((rows, half), BF16),
-            pltpu.VMEM((rows, half), BF16),
+            pltpu.VMEM((both, half), BF16),
+            pltpu.VMEM((both, half), BF16),
+            pltpu.VMEM((2, rows, 3 * rows), F32),
             dma((2 + 3 * CHUNKS,)),
             dma((2 + 3 * CHUNKS,)),
             dma((2 * CHUNKS,)),
@@ -406,7 +391,7 @@
             dma((CHUNKS + 1,)),
             dma((2 * CHUNKS,)),
             dma((2 * CHUNKS,)),
-            dma((6,)),
+            dma((6 + 2 * CHUNKS,)),
         ],
         compiler_params=pltpu.CompilerParams(
             collective_id=0, has_side_effects=True, vmem_limit_bytes=60 * 1024 * 1024
@@ -415,6 +400,7 @@
             flops=4_000_000_000, bytes_accessed=4_000_000, transcendentals=1_600_000
         ),
     )(linear_query, linear_key, values, window_query, window_key, selections(lanes))
+    return linear.astype(F32), window
 
 
 def solution(mesh):

time: 50.9 us -> 53.3 us (1.047)
  Pallas kernels: 47 us -> 49.6 us
  local copies, waits for them, and re-layouts: 3.15 us -> 0.8 us
  other arithmetic: 0 us -> 2.18 us
    pallas_call x1, Pallas kernels: 47 us -> 49.6 us  [on_device(): pl.pallas_call(functools.partial(kernel, pairs, rows, dim, heads), out_sh...]
    unnamed x4 -> x3, local copies, waits for them, and re-layouts: 3.15 us -> 0.8 us
    convert_element_type x0 -> x1, other arithmetic: none -> 2.18 us  [on_device(): return (linear.astype(F32), window)]
where the time goes in v3:
time: 53.3 us; the launch traced here: 53.2 us
  Pallas kernels  49.6 us (93%)
  other arithmetic  2.18 us (4%)
  local copies, waits for them, and re-layouts  0.8 us (2%)
  between operations  0.65 us (1%)
    pallas_call x1, Pallas kernels, on_device(): pl.pallas_call(functools.partial(kernel, pairs, rows, dim, heads), out_sh...  49.6 us
    convert_element_type x1, other arithmetic, on_device(): return (linear.astype(F32), window)  2.18 us

profile of v3, /device:TPU:24, one launch (start us, length us, event | category | flops | bytes accessed | tf_op | source)
XLA Modules:
  0.0 53.2 jit_solution(1944431360868928862)
XLA Ops:
  0.6 49.6 %shard_map.77 = (bf16[128,2048]{1,0:T(8,128)(2,1)}, bf16[128,2048]{1,0:T(8,128)(2,1)}) custom-call(bf16[128,256]{1,0:T(8,128)(2,1)} %lq_ref.1, bf16[128,256]{1,0:T(8,128)(2,1)} %lk_ref.1, bf16[128,2048]{1,0:T(8,128)(2,1)} %v_ref.1, bf16[128,2048]{1,0:T(8,128)(2,1)} %wq_ref.1, bf16[128,2048]{1,0:T(8,128)(2,1)} %wk_ref.1, ...), custom_call_target="tpu_custom_call" | custom-call | flops 4000000000 | bytes 4000000 | tf_op jit(solution)/shard_map/pallas_call | solution.py:356
  50.2 0.0 copy-start
  50.2 2.2 %convert_element_type.3 = f32[128,2048]{1,0:T(8,128)} convert(bf16[128,2048]{1,0:T(8,128)(2,1)} %get-tuple-element.4) | non-fusion elementwise | flops 262144 | bytes 1572864 | tf_op jit(solution)/shard_map/convert_element_type | solution.py:403
  52.4 0.0 copy-done
  52.4 0.8 %copy.9 = bf16[128,2048]{1,0:T(8,128)(2,1)} copy(bf16[128,2048]{1,0:T(8,128)(2,1)S(1)} %copy-done) | data formatting | bytes 1048576
Async XLA Ops:
  50.2 2.2 %copy-start = (bf16[128,2048]{1,0:T(8,128)(2,1)S(1)}, bf16[128,2048]{1,0:T(8,128)(2,1)}, u32[]{:S(2)}) copy-start(bf16[128,2048]{1,0:T(8,128)(2,1)} %get-tuple-element.9) | copy-start | bytes 1572868

commit v4 on v3

--- a/solution.py
+++ b/solution.py
@@ -44,7 +44,7 @@
     pairs, rows, dim, heads,
     lq_ref, lk_ref, v_ref, wq_ref, wk_ref, sel_in,
     lin_ref, win_ref,
-    sel_ref, lq2, lk2, v2, q2, k2, pv, pk, num, den, state, norm, state_in, norm_in, state_out, norm_out,
+    sel_ref, lqs, lks, vs, qs, ks, qf, lq2, lk2, v2, q2, k2, pv, pk, num, den, state, norm, state_in, norm_in, state_out, norm_out,
     lin_b, win_b, bias,
     xs, xr, zs, zr, ys, yr, cs, cr, rs, rr, ls,
 ):
@@ -68,11 +68,32 @@
     def own_cols(c):
         return pl.ds(pl.multiple_of(par * half + c * width, width), width)
 
-    def other_cols(c):
-        return pl.ds(pl.multiple_of(other * half + c * width, width), width)
-
     def cols(c):
         return pl.ds(c * width if isinstance(c, int) else pl.multiple_of(c * width, width), width)
+
+    small_other = pl.ds(pl.multiple_of(other * lanes, lanes), lanes)
+    small_own = pl.ds(pl.multiple_of(par * lanes, lanes), lanes)
+    all_own = pl.ds(pl.multiple_of(par * half, half), half)
+    all_other = pl.ds(pl.multiple_of(other * half, half), half)
+
+    def local(src, dst, at):
+        return pltpu.make_async_copy(src, dst, ls.at[at])
+
+    fetched = [
+        local(lk_ref.at[:, small_other], lks, 0),
+        local(lq_ref.at[:, small_other], lqs, 1),
+        local(v_ref.at[:, all_other], vs, 2),
+        local(v_ref.at[:, all_own], v2.at[mine, :], 3),
+        local(wk_ref.at[:, all_other], ks, 4),
+        local(wk_ref.at[:, all_own], k2.at[mine, :], 5),
+        local(wq_ref.at[:, all_other], qs, 6),
+        local(wq_ref.at[:, all_own], q2.at[mine, :], 7),
+        local(lk_ref.at[:, small_own], lk2.at[mine, :], 8),
+        local(lq_ref.at[:, small_own], lq2.at[mine, :], 9),
+        local(sel_in, sel_ref, 10),
+    ]
+    for copy in fetched:
+        copy.start()
 
     barrier = pltpu.get_barrier_semaphore()
     pl.semaphore_signal(barrier, inc=1, device_id=partner, device_id_type=MESH)
@@ -93,34 +114,31 @@
             device_id=where, device_id_type=MESH,
         )
 
-    small_other = pl.ds(pl.multiple_of(other * lanes, lanes), lanes)
-    small_own = pl.ds(pl.multiple_of(par * lanes, lanes), lanes)
-
     def x_lk():
-        return remote(lk_ref.at[:, small_other], lk2.at[mine, :], xs.at[0], xr.at[0], partner)
+        return remote(lks, lk2.at[mine, :], xs.at[0], xr.at[0], partner)
 
     def x_lq():
-        return remote(lq_ref.at[:, small_other], lq2.at[mine, :], xs.at[1], xr.at[1], partner)
+        return remote(lqs, lq2.at[mine, :], xs.at[1], xr.at[1], partner)
 
     def x_copy(src, dst, slot, c):
         at = 2 + slot * CHUNKS + c
-        return remote(src.at[:, other_cols(c)], dst.at[mine, cols(c)], xs.at[at], xr.at[at], partner)
+        return remote(src.at[:, cols(c)], dst.at[mine, cols(c)], xs.at[at], xr.at[at], partner)
 
     def x_v(c):
-        return x_copy(v_ref, v2, 0, c)
+        return x_copy(vs, v2, 0, c)
 
     def x_k(c):
-        return x_copy(wk_ref, k2, 1, c)
+        return x_copy(ks, k2, 1, c)
 
     def x_q(c):
-        return x_copy(wq_ref, q2, 2, c)
+        return x_copy(qs, q2, 2, c)
 
     def z_v(c):
-        return remote(v_ref.at[:, own_cols(c)], pv.at[mine, cols(c)], zs.at[c], zr.at[c], ahead)
+        return remote(v2.at[mine, cols(c)], pv.at[mine, cols(c)], zs.at[c], zr.at[c], ahead)
 
     def z_k(c):
         at = CHUNKS + c
-        return remote(wk_ref.at[:, own_cols(c)], pk.at[mine, cols(c)], zs.at[at], zr.at[at], ahead)
+        return remote(k2.at[mine, cols(c)], pk.at[mine, cols(c)], zs.at[at], zr.at[at], ahead)
 
     def y_v(c):
         return remote(v2.at[theirs, cols(c)], pv.at[theirs, cols(c)], ys.at[c], yr.at[c], ahead)
@@ -142,15 +160,14 @@
         at = CHUNKS + c
         return remote(win_b.at[theirs, cols(c)], win_ref.at[:, own_cols(c)], rs.at[at], rr.at[at], partner)
 
-    def local(src, dst, at):
-        return pltpu.make_async_copy(src, dst, ls.at[at])
-
     def l_lin(c):
-        return local(lin_b.at[mine, cols(c)], lin_ref.at[:, own_cols(c)], 6 + c)
+        return local(lin_b.at[mine, cols(c)], lin_ref.at[:, own_cols(c)], 11 + c)
 
     def l_win(c):
-        return local(win_b.at[mine, cols(c)], win_ref.at[:, own_cols(c)], 6 + CHUNKS + c)
-
+        return local(win_b.at[mine, cols(c)], win_ref.at[:, own_cols(c)], 11 + CHUNKS + c)
+
+    for copy in fetched:
+        copy.wait()
     x_lk().start()
     x_lq().start()
     for c in range(CHUNKS):
@@ -160,19 +177,6 @@
     def _():
         z_v(0).start()
 
-    small = [
-        local(sel_in, sel_ref, 0),
-        local(lk_ref.at[:, small_own], lk2.at[mine, :], 1),
-        local(lq_ref.at[:, small_own], lq2.at[mine, :], 2),
-    ]
-    all_own = pl.ds(pl.multiple_of(par * half, half), half)
-    large = [
-        local(v_ref.at[:, all_own], v2.at[mine, :], 3),
-        local(wk_ref.at[:, all_own], k2.at[mine, :], 4),
-        local(wq_ref.at[:, all_own], q2.at[mine, :], 5),
-    ]
-    for copy in small + large:
-        copy.start()
     for c in range(CHUNKS):
         x_k(c).start()
     for c in range(CHUNKS):
@@ -195,8 +199,6 @@
     for part in range(2):
         allowed = band & (k_at >= empty * (both - part * rows))
         bias[part] = jnp.where(allowed, 0.0, -1e30)
-    for copy in small + large:
-        copy.wait()
     x_lk().wait_recv()
     x_lq().wait_recv()
 
@@ -210,69 +212,111 @@
     row_right = jnp.where((feat_row >= PAIRS) & (feat_row <= ONE_ROW), 1.0, 0.0)
     norm_lane = lax.broadcasted_iota(jnp.int32, (FEATS, 128), 1)
 
-    def first(c, carry):
-        x_v(c).wait_recv()
-        for u in range(per):
-            head = c * per + u
-            at = pl.ds(pl.multiple_of(head * dim, dim), dim)
-            chosen = lane == head
-            keys = lk2[...]
-            key_m = jnp.where(chosen, keys.astype(F32), 0.0).astype(BF16)
-            query_m = jnp.where(chosen, lq2[...].astype(F32) * 0.25, 0.0).astype(BF16)
-            values = jnp.concatenate([v2[:, at], ones], axis=1)
-            feats = (dot_t(sel_ref[0], key_m) + row_left) * (dot_t(sel_ref[1], key_m) + row_right)
-            summed = dot(feats.astype(BF16), values)
-            state[head] = summed[:, :dim]
-            norm[...] += jnp.where(norm_lane == head, summed[:, dim:], 0.0)
-            a = dot_t(query_m, keys) + 1.0
-            weight = jnp.where(causal, a * a + 1.0, 0.0).astype(BF16)
-            mixed = dot(weight, values)
-            num[:, at] = mixed[:, :dim]
-            den[:, at] = mixed[:, dim:]
-
-        @pl.when(has_prev)
-        def _():
-            c_state(c).wait_recv()
-
-        @pl.when(has_next)
-        def _():
-            total = state_in[c].astype(F32) + state[pl.ds(c * per, per)]
-            state_out[c] = total.astype(state_out.dtype)
-            c_state(c).start()
-
-        @pl.when(has_next & (c < CHUNKS - 1))
-        def _():
-            z_v(c + 1).start()
-
-        return carry
-
-    lax.fori_loop(0, CHUNKS, first, 0)
-
-    @pl.when(has_prev)
-    def _():
-        c_norm().wait_recv()
-
-    @pl.when(has_next)
-    def _():
-        norm_out[...] = norm_in[...] + norm[...]
-        c_norm().start()
-
-    for c in range(CHUNKS):
-        x_k(c).wait_recv()
-
-        @pl.when(has_next)
-        def _():
-            y_v(c).start()
-            z_k(c).start()
-            y_k(c).start()
-
-    factor = dim ** -0.5 * 1.4426950408889634
     feat_lane = lax.broadcasted_iota(jnp.int32, (both, FEATS), 1)
     lane_left = jnp.where(feat_lane == ONE_ROW, 1.0, 0.0)
     lane_right = jnp.where((feat_lane >= PAIRS) & (feat_lane <= ONE_ROW), 2.0, 0.0)
+
+    def first(c, carry):
+        x_v(c).wait_recv()
+
+        @pl.when(has_next)
+        def _():
+            y_v(c).start()
+
+        todo = range(per)
+        keys = lk2[...]
+        head = [c * per + u for u in todo]
+        at = [pl.ds(pl.multiple_of(head[u] * dim, dim), dim) for u in todo]
+        key_m = [jnp.where(lane == head[u], keys.astype(F32), 0.0).astype(BF16) for u in todo]
+        query_m = [jnp.where(lane == head[u], lq2[...].astype(F32) * 0.25, 0.0).astype(BF16) for u in todo]
+        values = [jnp.concatenate([v2[:, at[u]], ones], axis=1) for u in todo]
+        left = [dot_t(sel_ref[0], key_m[u]) for u in todo]
+        right = [dot_t(sel_ref[1], key_m[u]) for u in todo]
+        a = [dot_t(query_m[u], keys) + 1.0 for u in todo]
+        feats = [((left[u] + row_left) * (right[u] + row_right)).astype(BF16) for u in todo]
+        summed = [dot(feats[u], values[u]) for u in todo]
+        weight = [jnp.where(causal, a[u] * a[u] + 1.0, 0.0).astype(BF16) for u in todo]
+        mixed = [dot(weight[u], values[u]) for u in todo]
+        for u in todo:
+            state[head[u]] = summed[u][:, :dim]
+            norm[...] += jnp.where(norm_lane == head[u], summed[u][:, dim:], 0.0)
+
+        @pl.when(has_next & (pair == 0))
+        def _():
+            for u in todo:
+                state_out[c, u] = summed[u][:, :dim].astype(state_out.dtype)
+            c_state(c).start()
+
+        @pl.when(has_next & (c < CHUNKS - 1))
+        def _():
+            z_v(c + 1).start()
+
+        left = [dot_t(query_m[u], sel_ref[0]) for u in todo]
+        right = [dot_t(query_m[u], sel_ref[2]) for u in todo]
+        for u in todo:
+            num[:, at[u]] = mixed[u][:, :dim]
+            den[:, at[u]] = mixed[u][:, dim:]
+            qf[head[u]] = ((left[u] + lane_left) * (right[u] + lane_right)).astype(BF16)
+        return carry
+
+    lax.fori_loop(0, CHUNKS, first, 0)
+
+    @pl.when(has_prev)
+    def _():
+        c_norm().wait_recv()
+
+    @pl.when(has_next)
+    def _():
+        norm_out[...] = norm_in[...] + norm[...]
+        c_norm().start()
+
+    def chain(c):
+        @pl.when(has_prev)
+        def _():
+            c_state(c).wait_recv()
+
+        @pl.when(has_prev & has_next)
+        def _():
+            total = state_in[c].astype(F32) + state[c * per : (c + 1) * per]
+            state_out[c] = total.astype(state_out.dtype)
+            c_state(c).start()
+
+    def bulk(c):
+        x_k(c).wait_recv()
+
+        @pl.when(has_next)
+        def _():
+            z_k(c).start()
+            y_k(c).start()
+
+    early = CHUNKS // 2
+    for c in range(early):
+        chain(c)
+
+    @pl.when(pair < 2)
+    def _():
+        for c in range(early, CHUNKS):
+            chain(c)
+
+    for c in range(early):
+        bulk(c)
+
+    @pl.when(pair < 2)
+    def _():
+        for c in range(early, CHUNKS):
+            bulk(c)
+
+    factor = dim ** -0.5 * 1.4426950408889634
     wide_ones = jnp.ones((span, dim), BF16)
 
     def second(c, carry):
+        @pl.when((c == 1) & (pair >= 2))
+        def _():
+            for late in range(early, CHUNKS):
+                chain(late)
+            for late in range(early, CHUNKS):
+                bulk(late)
+
         x_q(c).wait_recv()
 
         @pl.when(has_prev)
@@ -282,28 +326,33 @@
             y_v(c).wait_recv()
             y_k(c).wait_recv()
 
-        for u in range(per):
-            head = c * per + u
-            at = pl.ds(pl.multiple_of(head * dim, dim), dim)
-            for part in range(2):
-                begin = part * rows
-                keys = jnp.concatenate([pk[begin:, at], k2[: begin + rows, at]], axis=0)
-                values = jnp.concatenate([pv[begin:, at], v2[: begin + rows, at]], axis=0)
-                scores = dot_t(q2[begin : begin + rows, at], keys) * factor + bias[part]
-                largest = jnp.max(scores, axis=1, keepdims=True)
-                weight = jnp.exp2(scores - largest).astype(BF16)
-                mixed = dot(weight, jnp.concatenate([values, wide_ones], axis=1))
-                win_b[begin : begin + rows, at] = (mixed[:, :dim] / mixed[:, dim:]).astype(BF16)
-
-            query_m = jnp.where(lane == head, lq2[...].astype(F32) * 0.25, 0.0).astype(BF16)
-            feats = (dot_t(query_m, sel_ref[0]) + lane_left) * (dot_t(query_m, sel_ref[2]) + lane_right)
-            norm_col = jnp.sum(jnp.where(norm_lane == head, norm_in[...], 0.0), axis=1, keepdims=True)
+        todo = range(per)
+        head = [c * per + u for u in todo]
+        at = [pl.ds(pl.multiple_of(head[u] * dim, dim), dim) for u in todo]
+        both_parts = [(u, part, part * rows) for u in todo for part in range(2)]
+        scores = []
+        for u, part, begin in both_parts:
+            keys = jnp.concatenate([pk[begin:, at[u]], k2[: begin + rows, at[u]]], axis=0)
+            scores.append(dot_t(q2[begin : begin + rows, at[u]], keys))
+        scores = [scores[i] * factor + bias[part] for i, (u, part, begin) in enumerate(both_parts)]
+        largest = [jnp.max(score, axis=1, keepdims=True) for score in scores]
+        weights = [jnp.exp2(scores[i] - largest[i]).astype(BF16) for i in range(len(scores))]
+        mixed = []
+        for i, (u, part, begin) in enumerate(both_parts):
+            values = jnp.concatenate([pv[begin:, at[u]], v2[: begin + rows, at[u]]], axis=0)
+            mixed.append(dot(weights[i], jnp.concatenate([values, wide_ones], axis=1)))
+        added = []
+        for u in todo:
+            norm_col = jnp.sum(jnp.where(norm_lane == head[u], norm_in[...], 0.0), axis=1, keepdims=True)
             prior = jnp.concatenate(
                 [state_in[c, u].astype(BF16), jnp.broadcast_to(norm_col, (FEATS, dim)).astype(BF16)], axis=1
             )
-            added = dot(feats.astype(BF16), prior)
-            linear = (num[:, at] + added[:, :dim]) / (den[:, at] + added[:, dim:])
-            lin_b[:, at] = linear.astype(BF16)
+            added.append(dot(qf[head[u]], prior))
+        for i, (u, part, begin) in enumerate(both_parts):
+            win_b[begin : begin + rows, at[u]] = (mixed[i][:, :dim] / mixed[i][:, dim:]).astype(BF16)
+        for u in todo:
+            linear = (num[:, at[u]] + added[u][:, :dim]) / (den[:, at[u]] + added[u][:, dim:])
+            lin_b[:, at[u]] = linear.astype(BF16)
         r_lin(c).start()
         r_win(c).start()
         l_lin(c).start()
@@ -363,6 +412,12 @@
         out_specs=(pl.BlockSpec(memory_space=pl.ANY),) * 2,
         scratch_shapes=[
             pltpu.VMEM((3, FEATS, lanes), BF16),
+            pltpu.VMEM((rows, lanes), BF16),
+            pltpu.VMEM((rows, lanes), BF16),
+            pltpu.VMEM((rows, half), BF16),
+            pltpu.VMEM((rows, half), BF16),
+            pltpu.VMEM((rows, half), BF16),
+            pltpu.VMEM((half_heads, both, FEATS), BF16),
             pltpu.VMEM((both, lanes), BF16),
             pltpu.VMEM((both, lanes), BF16),
             pltpu.VMEM((both, half), BF16),
@@ -391,7 +446,7 @@
             dma((CHUNKS + 1,)),
             dma((2 * CHUNKS,)),
             dma((2 * CHUNKS,)),
-            dma((6 + 2 * CHUNKS,)),
+            dma((11 + 2 * CHUNKS,)),
         ],
         compiler_params=pltpu.CompilerParams(
             collective_id=0, has_side_effects=True, vmem_limit_bytes=60 * 1024 * 1024

time: 53.3 us -> 56.2 us (1.054)
  Pallas kernels: 49.6 us -> 52 us
    pallas_call x1, Pallas kernels: 49.6 us -> 52 us  [on_device(): pl.pallas_call(functools.partial(kernel, pairs, rows, dim, heads), out_sh...]
where the time goes in v4:
time: 56.2 us; the launch traced here: 55.7 us
  Pallas kernels  52 us (93%)
  other arithmetic  2.18 us (4%)
  local copies, waits for them, and re-layouts  0.8 us (1%)
  between operations  0.65 us (1%)
    pallas_call x1, Pallas kernels, on_device(): pl.pallas_call(functools.partial(kernel, pairs, rows, dim, heads), out_sh...  52 us
    convert_element_type x1, other arithmetic, on_device(): return (linear.astype(F32), window)  2.18 us

profile of v4, /device:TPU:24, one launch (start us, length us, event | category | flops | bytes accessed | tf_op | source)
XLA Modules:
  0.0 55.7 jit_solution(4046819510723680884)
XLA Ops:
  0.6 52.0 %shard_map.77 = (bf16[128,2048]{1,0:T(8,128)(2,1)}, bf16[128,2048]{1,0:T(8,128)(2,1)}) custom-call(bf16[128,256]{1,0:T(8,128)(2,1)} %lq_ref.1, bf16[128,256]{1,0:T(8,128)(2,1)} %lk_ref.1, bf16[128,2048]{1,0:T(8,128)(2,1)} %v_ref.1, bf16[128,2048]{1,0:T(8,128)(2,1)} %wq_ref.1, bf16[128,2048]{1,0:T(8,128)(2,1)} %wk_ref.1, ...), custom_call_target="tpu_custom_call" | custom-call | flops 4000000000 | bytes 4000000 | tf_op jit(solution)/shard_map/pallas_call | solution.py:405
  52.7 0.0 copy-start
  52.7 2.2 %convert_element_type.3 = f32[128,2048]{1,0:T(8,128)} convert(bf16[128,2048]{1,0:T(8,128)(2,1)} %get-tuple-element.4) | non-fusion elementwise | flops 262144 | bytes 1572864 | tf_op jit(solution)/shard_map/convert_element_type | solution.py:458
  54.9 0.0 copy-done
  54.9 0.8 %copy.9 = bf16[128,2048]{1,0:T(8,128)(2,1)} copy(bf16[128,2048]{1,0:T(8,128)(2,1)S(1)} %copy-done) | data formatting | bytes 1048576
Async XLA Ops:
  52.7 2.2 %copy-start = (bf16[128,2048]{1,0:T(8,128)(2,1)S(1)}, bf16[128,2048]{1,0:T(8,128)(2,1)}, u32[]{:S(2)}) copy-start(bf16[128,2048]{1,0:T(8,128)(2,1)} %get-tuple-element.9) | copy-start | bytes 1572868
